TPU v7x, 32 devices: a whole 2x2x4 slice. The times are simulated.
32 devices in a mesh: fleet: 2 (over x), leaf: 16 (over z, y, core).
Axes of the slice: x: 2, y: 2, z: 4, core: 2. Of those that a mesh axis runs over, the one named last changes fastest.
Arguments:
- points: float32 [16, 196608], P(None, ('fleet', 'leaf')), parts along dimension 1, may hold values from -6 to 6
- charges: float32 [16, 196608], P(None, ('fleet', 'leaf')), parts along dimension 1, may hold values from -6 to 6
- inv_scale: float32 [32], P('fleet'), parts along dimension 0, may hold values from 0.25 to 0.75
- order: int32 [196608], P(('fleet', 'leaf')), parts along dimension 0, may hold values from 0 to 98303, as said below
- near_list: int32 [192, 3], P(('fleet', 'leaf')), parts along dimension 0, may hold values from 0 to 95, as said below
- near_count: int32 [192], P(('fleet', 'leaf')), parts along dimension 0, may hold values from 2 to 3, as said below
- far_list: int32 [192, 6], P(('fleet', 'leaf')), parts along dimension 0, may hold values from 0 to 95, as said below
- skel_idx: int32 [192, 128], P(('fleet', 'leaf')), parts along dimension 0, may hold values from 0 to 1023, as said below
- interp: bfloat16 [128, 196608], P(None, ('fleet', 'leaf')), parts along dimension 1, may hold values from -0.1875 to 0.1875
- group_map: bfloat16 [24576, 128], P(('fleet', 'leaf')), parts along dimension 0, may hold values from -0.375 to 0.375
- parent_map: bfloat16 [512, 128], P('fleet'), parts along dimension 0, may hold values from -0.4375 to 0.4375
Outputs:
- potential: float32 [16, 196608], P(None, ('fleet', 'leaf')), parts along dimension 1
There are 2 independent parts, one for each index of `fleet`. A program takes and returns all parts, laid end to end along the dimension named above; each array names one. Nothing has to cross between parts.
Inputs may be any that keep to these rules, and one draw needn't show every extreme that they name: order maps the 6144 slots of each group to the points of that same group, each once. `near_list`: each entry names a leaf of the leaf's own group or of the group just before or after it; the used slots of a list are distinct. `near_count`: the first leaf of every group uses all 3 slots. `far_list`: distinct leaves of the leaf's own group or of the group just before or after it. `skel_idx`: the slots of one leaf are distinct.
All inputs are finite; a program needn't handle non-finite values.
Results may differ from a plain program's by a relative error of at most 0.0044.
Values sent between devices are 32-bit elements; how exact they have to be, the bound alone decides.
No kernel may reach another device: no remote copies, remote signals or barrier semaphores. Data moves between devices by JAX's collectives and lax.ppermute only.
A program may use at most 64 MiB of HBM per device.

v0:
```python
import functools
import math

import jax
import jax.numpy as jnp
from jax import lax
from jax.experimental import pallas as pl
from jax.experimental.pallas import tpu as pltpu
from jax.sharding import PartitionSpec as P

BF = jnp.bfloat16
F32 = jnp.float32
LANES = 128
BLOCK = 256
ROWS = 512
VMEM = pl.BlockSpec(memory_space=pltpu.VMEM)
SMEM = pl.BlockSpec(memory_space=pltpu.SMEM)


def params():
    return pltpu.CompilerParams(vmem_limit_bytes=48 * 2**20)


def halves(z):
    hi = z.astype(BF)
    return hi, (z - hi.astype(F32)).astype(BF)


def stacked_rows(z):
    hi, mid = halves(z)
    norm = -0.5 * jnp.sum(z * z, 0, keepdims=True)
    n1 = norm.astype(BF).astype(F32)
    n2 = (norm - n1).astype(BF).astype(F32)
    n3 = norm - n1 - n2
    shape = (16, z.shape[1])
    row = lax.broadcasted_iota(jnp.int32, shape, 0)

    def extra(first):
        out = jnp.where((row >= 3 - first) & (row < 6 - first), 1.0, 0.0)
        for i, piece in enumerate((n1, n2, n3)):
            out = jnp.where(row == first + i, jnp.broadcast_to(piece, shape), out)
        return out.astype(BF)

    source = jnp.concatenate([hi, mid, hi, mid, extra(3)], 0)
    target = jnp.concatenate([hi, hi, mid, mid, extra(0)], 0)
    return source, target


def tile_of(source, target):
    e = lax.dot_general(source, target, (((0,), (0,)), ((), ())), preferred_element_type=F32)
    return jnp.exp2(e).astype(BF)


def dot_t(a, b):
    return lax.dot_general(a, b, (((1,), (1,)), ((), ())), preferred_element_type=F32)


def dot(a, b):
    return jnp.dot(a, b, preferred_element_type=F32)


def one_hot(low, size):
    rows = lax.broadcasted_iota(jnp.int32, (size, low.shape[1]), 0)
    return (rows == low).astype(F32).astype(BF)


def pick_lanes(blocks, index):
    rows = blocks[0].shape[0]
    parts = []
    for top in range(0, rows, 8):
        idx = jnp.broadcast_to(index, (8, LANES))
        high, low = idx >> 7, idx & (LANES - 1)
        out = jnp.zeros((8, LANES), F32)
        for k, block in enumerate(blocks):
            got = jnp.take_along_axis(block[top : top + 8], low, axis=1, mode="promise_in_bounds")
            out = jnp.where(high == k, got, out)
        parts.append(out)
    return jnp.concatenate(parts, 0)


def index_kernel(order_ref, out_ref):
    out_ref[...] = order_ref[...] - lax.axis_index("leaf") * order_ref.shape[1]


def local_index(order):
    return pl.pallas_call(
        index_kernel,
        out_shape=jax.ShapeDtypeStruct(order.shape, jnp.int32),
        in_specs=[VMEM],
        out_specs=VMEM,
        compiler_params=params(),
        cost_estimate=pl.CostEstimate(flops=10**9, bytes_accessed=10**6, transcendentals=0),
        name="local_index",
    )(order)


def prepare_kernel(
    scale_ref, points_ref, charges_ref, order_ref, skel_ref, map_ref, interp_ref,
    pack_ref, source_ref, target_ref, zs_ref, bs_ref,
):
    feats, total = points_ref.shape
    rhs = charges_ref.shape[0]
    leaves, rank = skel_ref.shape
    width = total // leaves
    blocks = total // BLOCK
    shift = BLOCK.bit_length() - 1
    row = lax.broadcasted_iota(jnp.int32, (feats, LANES), 0)
    scale = jnp.zeros((feats, LANES), F32)
    for r in range(feats):
        scale = jnp.where(row == r, scale_ref[r], scale)
    scale = scale[:, :1] * math.sqrt(math.log2(math.e))
    for k in range(blocks):
        span = slice(k * BLOCK, (k + 1) * BLOCK)
        hi, mid = halves(points_ref[:, span] * scale)
        zs_ref[k * feats : (k + 1) * feats, :BLOCK] = hi
        zs_ref[k * feats : (k + 1) * feats, BLOCK:] = mid
        bs_ref[k * rhs : (k + 1) * rhs, :] = charges_ref[:, span].astype(BF)

    def step(j, carry):
        start = pl.multiple_of(j * width, width)
        index = order_ref[:, pl.ds(start, width)]
        hot = one_hot(index & (BLOCK - 1), BLOCK)
        yz = dot(zs_ref[...], jnp.concatenate([hot, hot], 0))
        yb = dot(bs_ref[...], hot)
        high = jnp.broadcast_to(index >> shift, (feats, width))
        az = jnp.zeros((feats, width), F32)
        ab = jnp.zeros((rhs, width), F32)
        for k in range(blocks):
            mask = high == k
            az = jnp.where(mask, yz[k * feats : (k + 1) * feats], az)
            ab = jnp.where(mask, yb[k * rhs : (k + 1) * rhs], ab)
        pack_ref[:feats, pl.ds(start, width)] = az
        pack_ref[feats:, pl.ds(start, width)] = ab
        source, target = stacked_rows(az)
        source_ref[:, pl.ds(start, width)] = source
        target_ref[:, pl.ds(start, width)] = target
        return carry

    lax.fori_loop(0, leaves, step, 0)
    group_q = jnp.zeros((rhs, rank), F32)
    for leaf in range(leaves):
        span = slice(leaf * width, (leaf + 1) * width)
        out = slice(total + leaf * rank, total + (leaf + 1) * rank)
        columns = [
            pack_ref[:feats, leaf * width + k : leaf * width + k + LANES]
            for k in range(0, width, LANES)
        ]
        pack_ref[:feats, out] = pick_lanes(columns, skel_ref[leaf : leaf + 1, :])
        charge = dot_t(pack_ref[feats:, span].astype(BF), interp_ref[:, span]).astype(BF)
        pack_ref[feats:, out] = charge.astype(F32)
        group_q += dot(charge, map_ref[leaf * rank : (leaf + 1) * rank, :])
    columns = [pack_ref[:feats, total + k : total + k + LANES] for k in range(0, leaves * rank, LANES)]
    node = slice(total + leaves * rank, total + (leaves + 1) * rank)
    pack_ref[:feats, node] = pick_lanes(
        columns, lax.broadcasted_iota(jnp.int32, (1, rank), 1) * leaves
    )
    pack_ref[feats:, node] = group_q


def prepare(inv_scale, points, charges, order, skel_idx, interp, group_map):
    feats, total = points.shape
    rhs = charges.shape[0]
    leaves, rank = skel_idx.shape
    blocks = total // BLOCK
    stack = 4 * feats + 16
    return pl.pallas_call(
        prepare_kernel,
        out_shape=(
            jax.ShapeDtypeStruct((feats + rhs, total + (leaves + 1) * rank), F32),
            jax.ShapeDtypeStruct((stack, total), BF),
            jax.ShapeDtypeStruct((stack, total), BF),
        ),
        in_specs=[SMEM] + [VMEM] * 6,
        out_specs=(VMEM,) * 3,
        scratch_shapes=[
            pltpu.VMEM((blocks * feats, 2 * BLOCK), BF),
            pltpu.VMEM((blocks * rhs, BLOCK), BF),
        ],
        compiler_params=params(),
        name="prepare",
    )(inv_scale, points, charges, order, skel_idx, group_map, interp)


def region_of(leaf_id, leaves):
    device = lax.axis_index("leaf")
    rel = leaf_id - (device - 1) * leaves
    side = (rel >= leaves).astype(jnp.int32) + (rel >= 2 * leaves).astype(jnp.int32)
    odd = device & 1
    region = jnp.where(side == 1, 0, jnp.where(side == 2 * (1 - odd), 1, 2))
    return region, rel - side * leaves


def near_kernel(list_ref, count_ref, target_ref, src_ref, *refs, feats, region, limits, first, after):
    refs = list(refs)
    acc_ref = None if first else refs.pop(0)
    if after:
        refs.pop(0)
    if region == 0:
        stack_ref, out_ref = refs
    else:
        out_ref, stack_ref = refs
    out_ref[...] = jnp.zeros_like(out_ref) if first else acc_ref[...]
    slots, leaves = list_ref.shape
    width = target_ref.shape[1] // leaves
    low, high = limits

    def per_leaf(leaf, seen):
        start = pl.multiple_of(leaf * width, width)

        def per_slot(slot, seen):
            found, place = region_of(list_ref[slot, leaf], leaves)
            match = found == region

            @pl.when(match & (seen >= low) & (seen < high))
            def _():
                at = pl.multiple_of(place * width, width)
                if region == 0:
                    source = stack_ref[:, pl.ds(at, width)]
                else:
                    source, _ = stacked_rows(src_ref[:feats, pl.ds(at, width)])
                    stack_ref[...] = source
                    source = stack_ref[...]
                charge = src_ref[feats:, pl.ds(at, width)].astype(BF)
                target = target_ref[:, pl.ds(start, width)]
                acc = out_ref[:, pl.ds(start, width)]
                for row in range(0, width, ROWS):
                    tile = tile_of(source[:, row : row + ROWS], target)
                    acc = acc + dot(charge[:, row : row + ROWS], tile)
                out_ref[:, pl.ds(start, width)] = acc

            return seen + match.astype(jnp.int32)

        return lax.fori_loop(0, count_ref[leaf], per_slot, seen)

    lax.fori_loop(0, leaves, per_leaf, jnp.int32(0))


def near_part(near_list, near_count, targets, source, acc, after, stack, feats, region, limits, tiles):
    slots, leaves = near_list.shape
    rhs = source.shape[0] - feats
    total = targets.shape[1]
    width = total // leaves
    extra = [value for value in (acc, after, stack) if value is not None]
    return pl.pallas_call(
        functools.partial(
            near_kernel,
            feats=feats,
            region=region,
            limits=limits,
            first=acc is None,
            after=after is not None,
        ),
        out_shape=jax.ShapeDtypeStruct((rhs, total), F32),
        in_specs=[SMEM, SMEM] + [VMEM] * (2 + len(extra)),
        out_specs=VMEM,
        scratch_shapes=[] if region == 0 else [pltpu.VMEM((targets.shape[0], width), BF)],
        compiler_params=params(),
        cost_estimate=pl.CostEstimate(
            flops=tiles * width * width * 1024,
            bytes_accessed=tiles * 48 * width * 4,
            transcendentals=tiles * width * width,
        ),
        name=f"near_{region}_{limits[0]}",
    )(near_list, near_count, targets, source, *extra)


def climb(nodes, base, levels, parent_map, feats, top=False):
    device = lax.axis_index("leaf")
    rank = nodes[0].shape[1]
    lane = lax.broadcasted_iota(jnp.int32, (1, rank), 1)
    inters = []
    for level in range(levels):
        own, other = nodes[0], nodes[1]
        source, _ = stacked_rows(other[:feats])
        _, target = stacked_rows(own[:feats])
        inters.append(dot(other[feats:].astype(BF), tile_of(source, target)))
        if top and level == levels - 1:
            break
        odd = (device >> (base + level)) & 1
        parents = []
        for k in range(0, len(nodes), 2):
            left = jnp.where(odd == 1, nodes[k + 1], nodes[k])
            right = jnp.where(odd == 1, nodes[k], nodes[k + 1])
            z = pick_lanes([left[:feats], right[:feats]], lane * 2)
            q = dot(left[feats:].astype(BF), parent_map[:rank, :])
            q += dot(right[feats:].astype(BF), parent_map[rank:, :])
            parents.append(jnp.concatenate([z, q], 0))
        nodes = parents
    return inters, nodes[0]


def climb_kernel(*refs, base, levels, feats):
    count = 2**levels
    rank = refs[count].shape[1]
    nodes = [ref[:, ref.shape[1] - rank :] for ref in refs[:count]]
    inters, node = climb(nodes, base, levels, refs[count][...], feats)
    for ref, value in zip(refs[count + 1 :], inters + [node]):
        ref[...] = value


def climb_stage(nodes, base, levels, parent_map, feats):
    rows, rank = nodes[0].shape[0], parent_map.shape[1]
    small = jax.ShapeDtypeStruct((rows - feats, rank), F32)
    outs = pl.pallas_call(
        functools.partial(climb_kernel, base=base, levels=levels, feats=feats),
        out_shape=(small,) * levels + (jax.ShapeDtypeStruct((rows, rank), F32),),
        in_specs=[VMEM] * (len(nodes) + 1),
        out_specs=(VMEM,) * (levels + 1),
        compiler_params=params(),
        name=f"climb_{base}",
    )(*nodes, parent_map)
    return list(outs[:-1]), outs[-1]


def finish_kernel(
    far_ref, near_ref, own_ref, chip_ref, beyond_ref, interp_ref, order_ref, map_ref, parent_ref,
    *refs, feats, base, levels, done,
):
    count = 2**levels
    nodes = [ref[...] for ref in refs[:count]]
    inters = [ref[...] for ref in refs[count : count + done]]
    out_ref, skel_ref, charge_ref, acc_ref = refs[count + done :]
    leaves, slots = far_ref.shape
    rank = interp_ref.shape[0]
    rhs, total = near_ref.shape
    width = total // leaves
    device = lax.axis_index("leaf")
    parent_map = parent_ref[...]
    fresh, _ = climb(nodes, base, levels, parent_map, feats, top=True)
    inters = inters + fresh
    down = inters[-1]
    for level in range(len(inters) - 2, -1, -1):
        spread = dot_t(down.astype(BF), parent_map)
        odd = (device >> level) & 1
        down = inters[level] + jnp.where(odd == 1, spread[:, rank:], spread[:, :rank])
    leaf_out = dot_t(down.astype(BF), map_ref[...])

    targets = []
    for region, ref in enumerate((own_ref, chip_ref, beyond_ref)):
        skels = slice(total, total + leaves * rank)
        source, target = stacked_rows(ref[:feats, skels])
        charge = ref[feats:, skels].astype(BF)
        for leaf in range(leaves):
            span = slice(leaf * rank, (leaf + 1) * rank)
            skel_ref[region * leaves + leaf] = source[:, span]
            charge_ref[region * leaves + leaf] = charge[:, span]
            if region == 0:
                targets.append(target[:, span])
    pieces = []
    for leaf in range(leaves):
        field = leaf_out[:, leaf * rank : (leaf + 1) * rank]
        where = []
        for slot in range(slots):
            region, place = region_of(far_ref[leaf, slot], leaves)
            where.append(region * leaves + place)
        sources = jnp.concatenate([skel_ref[w] for w in where], 1)
        charges = jnp.concatenate([charge_ref[w] for w in where], 1)
        field += dot(charges, tile_of(sources, targets[leaf]))
        span = slice(leaf * width, (leaf + 1) * width)
        pieces.append(near_ref[:, span] + dot(field.astype(BF), interp_ref[:, span]))

    blocks = total // BLOCK
    shift = BLOCK.bit_length() - 1
    for leaf in range(leaves):
        index = order_ref[:, leaf * width : (leaf + 1) * width]
        hot = one_hot(index & (BLOCK - 1), BLOCK)
        high = jnp.broadcast_to(index >> shift, (rhs, width))
        hi, mid = halves(pieces[leaf])
        hi, mid = hi.astype(F32), mid.astype(F32)
        rows = []
        for k in range(blocks):
            mask = high == k
            rows.append(jnp.where(mask, hi, 0.0).astype(BF))
            rows.append(jnp.where(mask, mid, 0.0).astype(BF))
        part = dot_t(jnp.concatenate(rows, 0), hot)
        acc_ref[...] = part if leaf == 0 else acc_ref[...] + part
    for k in range(blocks):
        top = 2 * rhs * k
        out_ref[:, k * BLOCK : (k + 1) * BLOCK] = (
            acc_ref[top : top + rhs, :] + acc_ref[top + rhs : top + 2 * rhs, :]
        )


def finish(far_list, near, packs, interp, order, group_map, parent_map, nodes, inters, base, levels, feats):
    rhs, total = near.shape
    leaves = far_list.shape[0]
    rank = interp.shape[0]
    return pl.pallas_call(
        functools.partial(finish_kernel, feats=feats, base=base, levels=levels, done=len(inters)),
        out_shape=jax.ShapeDtypeStruct((rhs, total), F32),
        in_specs=[SMEM] + [VMEM] * (8 + len(nodes) + len(inters)),
        out_specs=VMEM,
        scratch_shapes=[
            pltpu.VMEM((3 * leaves, 4 * feats + 16, rank), BF),
            pltpu.VMEM((3 * leaves, rhs, rank), BF),
            pltpu.VMEM((total // BLOCK * 2 * rhs, BLOCK), F32),
        ],
        compiler_params=params(),
        name="finish",
    )(far_list, near, *packs, interp, order, group_map, parent_map, *nodes, *inters)


def body(
    points,
    charges,
    inv_scale,
    order,
    near_list,
    near_count,
    far_list,
    skel_idx,
    interp,
    group_map,
    parent_map,
):
    feats = points.shape[0]
    leaves = near_list.shape[0]
    devices = lax.axis_size("leaf")
    order = local_index(order.reshape(1, -1))
    near_list = near_list.T
    chip = [(i, i ^ 1) for i in range(devices)]
    beyond = []
    for i in range(1, devices - 1, 2):
        beyond += [(i, i + 1), (i + 1, i)]

    def relatives(node, base, levels):
        out = [node]
        for k in range(1, 2**levels):
            pairs = [(i, i ^ (k << base)) for i in range(devices)]
            out.append(lax.ppermute(node, "leaf", pairs))
        return out

    pack, sources, targets = prepare(
        inv_scale, points, charges, order, skel_idx, interp, group_map
    )

    def near(source, acc, after, region, limits, tiles):
        stack = sources if region == 0 else None
        return near_part(
            near_list, near_count, targets, source, acc, after, stack, feats, region, limits, tiles
        )

    every = near_list.shape[0] * leaves
    pack_chip = lax.ppermute(pack, "leaf", chip)
    pack_beyond = lax.ppermute(pack, "leaf", beyond)
    levels = devices.bit_length() - 1
    stages = [(1, 1)] + [(base, min(2, levels - base)) for base in range(2, levels, 2)]
    total = near(pack, None, None, 0, (0, 2), 2)
    inters, node = climb_stage([pack, pack_chip], 0, 1, parent_map, feats)
    nodes = relatives(node, *stages[0])
    total = near(pack, total, node, 0, (2, 4), 2)
    for stage, following in zip(stages[:-1], stages[1:]):
        fresh, node = climb_stage(nodes, *stage, parent_map, feats)
        inters += fresh
        nodes = relatives(node, *following)
    total = near(pack, total, node, 0, (4, every), 3)
    total = near(pack_chip, total, None, 1, (0, every), 6)
    total = near(pack_beyond, total, None, 2, (0, every), 6)
    packs = (pack, pack_chip, pack_beyond)
    return finish(
        far_list, total, packs, interp, order, group_map, parent_map, nodes, inters, *stages[-1], feats
    )


def solution(mesh):
    placed = (
        P(None, ("fleet", "leaf")),
        P(None, ("fleet", "leaf")),
        P("fleet"),
        P(("fleet", "leaf")),
        P(("fleet", "leaf"), None),
        P(("fleet", "leaf")),
        P(("fleet", "leaf"), None),
        P(("fleet", "leaf"), None),
        P(None, ("fleet", "leaf")),
        P(("fleet", "leaf"), None),
        P("fleet", None),
    )
    return jax.shard_map(
        body, mesh=mesh, in_specs=placed, out_specs=P(None, ("fleet", "leaf")), check_vma=False
    )
```

profile of v0, /device:TPU:0, one launch (start us, length us, event | category | flops | bytes accessed | tf_op | source)
XLA Modules:
  0.0 61.7 jit_solution(11125162962156809181)
XLA Ops:
  0.0 0.0 copy-start.8
  0.0 0.7 %copy-done.8 = s32[6144]{0:T(1024)S(1)} copy-done((s32[6144]{0:T(1024)S(1)}, s32[6144]{0:T(1024)}, u32[]{:S(2)}) %copy-start.8) | copy-done | bytes 24600
  0.7 0.0 copy-start
  0.7 0.0 copy-start.1
  0.7 0.0 copy-start.3
  0.7 0.0 copy-start.4
  0.7 0.0 copy-start.5
  0.8 0.0 copy-start.7
  0.8 1.4 %copy-done = bf16[128,6144]{1,0:T(8,128)(2,1)S(1)} copy-done((bf16[128,6144]{1,0:T(8,128)(2,1)S(1)}, bf16[128,6144]{1,0:T(8,128)(2,1)}, u32[]{:S(2)}) %copy-start) | copy-done | bytes 1572888
  2.1 0.0 copy-done.1
  2.1 0.1 copy-done.3
  2.3 0.1 copy-done.4
  2.4 0.0 copy-done.5
  2.4 0.0 copy-done.7
  2.4 0.0 copy-start.9
  2.4 0.0 copy-start.10
  2.4 6.6 %prepare.1 = (f32[32,7040]{1,0:T(8,128)S(1)}, bf16[80,6144]{1,0:T(8,128)(2,1)S(1)}, bf16[80,6144]{1,0:T(8,128)(2,1)S(1)}) custom-call(f32[16]{0:T(128)S(1)} %copy-done.7, f32[16,6144]{1,0:T(8,128)S(1)} %copy-done.3, f32[16,6144]{1,0:T(8,128)S(1)} %copy-done.4, s32[1,6144]{1,0:T(1,128)S(1)} %local_index.1.order_ref, s32[6,128]{1,0:T(8,128)S(1)} %copy-done.5, ...), custom_call_target="tpu_custom_call" | custom-call | tf_op jit(solution)/shard_map/prepare/pallas_call | solution.py:166
  9.0 0.5 collective-permute-start.1
  9.5 0.7 %collective-permute-start = (f32[32,7040]{1,0:T(8,128)S(1)}, f32[32,7040]{1,0:T(8,128)S(1)}, u32[]{:S(2)}, u32[]{:S(2)}) collective-permute-start(f32[32,7040]{1,0:T(8,128)S(1)} %get-tuple-element.13.src_ref.refs_0_.own_ref), channel_id=1, source_target_pairs={{1,2},{2,1},{3,4},{4,3},{5,6},{6,5},{7,8},{8,7},{9,10},{10,9},{11,... | collective-permute-start | bytes 2703368 | tf_op jit(solution)/shard_map/ppermute | solution.py:445
  10.2 0.0 copy-done.9
  10.2 0.0 copy-done.10
  10.2 0.0 copy-start.2
  10.2 2.9 %near_0_0.1.refs_0_ = f32[16,6144]{1,0:T(8,128)S(1)} custom-call(s32[3,6]{1,0:T(4,128)S(1)} %bitcast.3, s32[6]{0:T(128)S(1)} %copy-done.10, bf16[80,6144]{1,0:T(8,128)(2,1)S(1)} %get-tuple-element.12.target_ref, f32[32,7040]{1,0:T(8,128)S(1)} %get-tuple-element.13.src_ref.refs_0_.own_ref, bf16[80,6144]{1,0:T(8,128)(2,1)S(1)} %get-tuple-element.14.refs_0_.refs_2_), custom_call_target="tpu_custom_call" | custom-call | flops 2147483648 | bytes 393216 | tf_op jit(solution)/shard_map/near_0_0/pallas_call | solution.py:244
  13.1 0.0 collective-permute-done.1.refs_1_.src_ref.chip_ref
  13.1 0.0 copy-done.2
  13.1 0.3 climb_0.1
  13.4 3.7 %collective-permute-start.2 = (f32[32,128]{1,0:T(8,128)S(1)}, f32[32,128]{1,0:T(8,128)S(1)}, u32[]{:S(2)}, u32[]{:S(2)}) collective-permute-start(f32[32,128]{1,0:T(8,128)S(1)} %get-tuple-element.15.refs_1_.refs_0_), channel_id=1, source_target_pairs={{0,2},{1,3},{2,0},{3,1},{4,6},{5,7},{6,4},{7,5},{8,10},{9,11},{10,... | collective-permute-start | bytes 49160 | tf_op jit(solution)/shard_map/ppermute | solution.py:430
  17.1 2.9 %near_0_2.1.refs_0_ = f32[16,6144]{1,0:T(8,128)S(1)} custom-call(s32[3,6]{1,0:T(4,128)S(1)} %bitcast.4, s32[6]{0:T(128)S(1)} %copy-done.10, bf16[80,6144]{1,0:T(8,128)(2,1)S(1)} %get-tuple-element.12.target_ref, f32[32,7040]{1,0:T(8,128)S(1)} %get-tuple-element.13.src_ref.refs_0_.own_ref, f32[16,6144]{1,0:T(8,128)S(1)} %near_0_0.1.refs_0_, ...), custom_call_target="tpu_custom_call" | custom-call | flops 2147483648 | bytes 393216 | tf_op jit(solution)/shard_map/near_0_2/pallas_call | solution.py:244
  20.0 5.4 %collective-permute-done.2.refs_1_ = f32[32,128]{1,0:T(8,128)S(1)} collective-permute-done((f32[32,128]{1,0:T(8,128)S(1)}, f32[32,128]{1,0:T(8,128)S(1)}, u32[]{:S(2)}, u32[]{:S(2)}) %collective-permute-start.2) | collective-permute-done | bytes 16416 | tf_op jit(solution)/shard_map/ppermute | solution.py:430
  25.4 0.3 climb_1.1
  25.7 13.9 %collective-permute-start.5 = (f32[32,128]{1,0:T(8,128)S(1)}, f32[32,128]{1,0:T(8,128)S(1)}, u32[]{:S(2)}, u32[]{:S(2)}) collective-permute-start(f32[32,128]{1,0:T(8,128)S(1)} %get-tuple-element.16.refs_1_.refs_0_), channel_id=1, source_target_pairs={{0,12},{1,13},{2,14},{3,15},{4,8},{5,9},{6,10},{7,11},{8,4},{9,5},... | collective-permute-start | bytes 49160 | tf_op jit(solution)/shard_map/ppermute | solution.py:430
  39.6 0.0 collective-permute-start.4
  39.6 0.6 collective-permute-start.3
  40.2 3.9 %near_0_4.1.refs_0_ = f32[16,6144]{1,0:T(8,128)S(1)} custom-call(s32[3,6]{1,0:T(4,128)S(1)} %bitcast.5, s32[6]{0:T(128)S(1)} %copy-done.10, bf16[80,6144]{1,0:T(8,128)(2,1)S(1)} %get-tuple-element.12.target_ref, f32[32,7040]{1,0:T(8,128)S(1)} %get-tuple-element.13.src_ref.refs_0_.own_ref, f32[16,6144]{1,0:T(8,128)S(1)} %near_0_2.1.refs_0_, ...), custom_call_target="tpu_custom_call" | custom-call | flops 3221225472 | bytes 589824 | tf_op jit(solution)/shard_map/near_0_4/pallas_call | solution.py:244
  44.1 8.7 %near_1_0.1.refs_0_ = f32[16,6144]{1,0:T(8,128)S(1)} custom-call(s32[3,6]{1,0:T(4,128)S(1)} %bitcast.6, s32[6]{0:T(128)S(1)} %copy-done.10, bf16[80,6144]{1,0:T(8,128)(2,1)S(1)} %get-tuple-element.12.target_ref, f32[32,7040]{1,0:T(8,128)S(1)} %collective-permute-done.1.refs_1_.src_ref.chip_ref, f32[16,6144]{1,0:T(8,128)S(1)} %near_0_4.1.refs_0_), custom_call_target="tpu_custom_call" | custom-call | flops 6442450944 | bytes 1179648 | tf_op jit(solution)/shard_map/near_1_0/pallas_call | solution.py:244
  52.7 0.0 copy-start.6
  52.7 0.0 collective-permute-done.src_ref.beyond_ref
  52.7 1.1 %near_2_0.1.near_ref = f32[16,6144]{1,0:T(8,128)S(1)} custom-call(s32[3,6]{1,0:T(4,128)S(1)} %bitcast.7, s32[6]{0:T(128)S(1)} %copy-done.10, bf16[80,6144]{1,0:T(8,128)(2,1)S(1)} %get-tuple-element.12.target_ref, f32[32,7040]{1,0:T(8,128)S(1)} %collective-permute-done.src_ref.beyond_ref, f32[16,6144]{1,0:T(8,128)S(1)} %near_1_0.1.refs_0_), custom_call_target="tpu_custom_call" | custom-call | flops 6442450944 | bytes 1179648 | tf_op jit(solution)/shard_map/near_2_0/pallas_call | solution.py:244
  53.8 0.0 collective-permute-done.5.refs_3_
  53.8 0.0 collective-permute-done.4.refs_2_
  53.8 0.0 collective-permute-done.3.refs_1_
  53.8 0.0 copy-done.6
  53.8 7.9 %finish.1 = f32[16,6144]{1,0:T(8,128)} custom-call(s32[6,6]{1,0:T(8,128)S(1)} %copy-done.6, f32[16,6144]{1,0:T(8,128)S(1)} %near_2_0.1.near_ref, f32[32,7040]{1,0:T(8,128)S(1)} %get-tuple-element.13.src_ref.refs_0_.own_ref, f32[32,7040]{1,0:T(8,128)S(1)} %collective-permute-done.1.refs_1_.src_ref.chip_ref, ...), custom_call_target="tpu_custom_call" | custom-call | tf_op jit(solution)/shard_map/finish/pallas_call | solution.py:388
  (1 shorter events, 0.0 us)
Async XLA Ops:
  0.0 0.7 %copy-start.8 = (s32[6144]{0:T(1024)S(1)}, s32[6144]{0:T(1024)}, u32[]{:S(2)}) copy-start(s32[6144]{0:T(1024)} %param.14) | copy-start | bytes 73732
  0.7 1.4 %copy-start = (bf16[128,6144]{1,0:T(8,128)(2,1)S(1)}, bf16[128,6144]{1,0:T(8,128)(2,1)}, u32[]{:S(2)}) copy-start(bf16[128,6144]{1,0:T(8,128)(2,1)} %interp_ref.3) | copy-start | bytes 4718596
  0.7 1.4 %copy-start.1 = (bf16[768,128]{1,0:T(8,128)(2,1)S(1)}, bf16[768,128]{1,0:T(8,128)(2,1)}, u32[]{:S(2)}) copy-start(bf16[768,128]{1,0:T(8,128)(2,1)} %map_ref.3) | copy-start | bytes 589828
  0.7 1.5 %copy-start.3 = (f32[16,6144]{1,0:T(8,128)S(1)}, f32[16,6144]{1,0:T(8,128)}, u32[]{:S(2)}) copy-start(f32[16,6144]{1,0:T(8,128)} %points_ref.1) | copy-start | bytes 1179652
  0.7 1.7 %copy-start.4 = (f32[16,6144]{1,0:T(8,128)S(1)}, f32[16,6144]{1,0:T(8,128)}, u32[]{:S(2)}) copy-start(f32[16,6144]{1,0:T(8,128)} %charges_ref.1) | copy-start | bytes 1179652
  0.7 1.7 %copy-start.5 = (s32[6,128]{1,0:T(8,128)S(1)}, s32[6,128]{1,0:T(8,128)}, u32[]{:S(2)}) copy-start(s32[6,128]{1,0:T(8,128)} %skel_ref.1) | copy-start | bytes 9220
  0.8 1.7 %copy-start.7 = (f32[16]{0:T(128)S(1)}, f32[16]{0:T(128)}, u32[]{:S(2)}) copy-start(f32[16]{0:T(128)} %scale_ref.1) | copy-start | bytes 196
  2.4 7.8 %copy-start.9 = (s32[6,3]{0,1:T(4,128)S(1)}, s32[6,3]{0,1:T(4,128)}, u32[]{:S(2)}) copy-start(s32[6,3]{0,1:T(4,128)} %param.15) | copy-start | bytes 220
  2.4 7.8 %copy-start.10 = (s32[6]{0:T(128)S(1)}, s32[6]{0:T(128)}, u32[]{:S(2)}) copy-start(s32[6]{0:T(128)} %count_ref.9) | copy-start | bytes 76
  9.0 4.1 %collective-permute-start.1 = (f32[32,7040]{1,0:T(8,128)S(1)}, f32[32,7040]{1,0:T(8,128)S(1)}, u32[]{:S(2)}, u32[]{:S(2)}) collective-permute-start(f32[32,7040]{1,0:T(8,128)S(1)} %get-tuple-element.13.src_ref.refs_0_.own_ref), channel_id=1, source_target_pairs={{0,1},{1,0},{2,3},{3,2},{4,5},{5,4},{6,7},{7,6},{8,9},{9,8},{10,11... | collective-permute-start | bytes 2703368 | tf_op jit(solution)/shard_map/ppermute | solution.py:444
  9.5 43.3 %collective-permute-start = (f32[32,7040]{1,0:T(8,128)S(1)}, f32[32,7040]{1,0:T(8,128)S(1)}, u32[]{:S(2)}, u32[]{:S(2)}) collective-permute-start(f32[32,7040]{1,0:T(8,128)S(1)} %get-tuple-element.13.src_ref.refs_0_.own_ref), channel_id=1, source_target_pairs={{1,2},{2,1},{3,4},{4,3},{5,6},{6,5},{7,8},{8,7},{9,10},{10,9},{11,... | collective-permute-start | bytes 2703368 | tf_op jit(solution)/shard_map/ppermute | solution.py:445
  10.2 2.9 %copy-start.2 = (bf16[256,128]{1,0:T(8,128)(2,1)S(1)}, bf16[256,128]{1,0:T(8,128)(2,1)}, u32[]{:S(2)}) copy-start(bf16[256,128]{1,0:T(8,128)(2,1)} %parent_ref.1) | copy-start | bytes 196612
  13.4 12.0 %collective-permute-start.2 = (f32[32,128]{1,0:T(8,128)S(1)}, f32[32,128]{1,0:T(8,128)S(1)}, u32[]{:S(2)}, u32[]{:S(2)}) collective-permute-start(f32[32,128]{1,0:T(8,128)S(1)} %get-tuple-element.15.refs_1_.refs_0_), channel_id=1, source_target_pairs={{0,2},{1,3},{2,0},{3,1},{4,6},{5,7},{6,4},{7,5},{8,10},{9,11},{10,... | collective-permute-start | bytes 49160 | tf_op jit(solution)/shard_map/ppermute | solution.py:430
  25.7 28.1 %collective-permute-start.5 = (f32[32,128]{1,0:T(8,128)S(1)}, f32[32,128]{1,0:T(8,128)S(1)}, u32[]{:S(2)}, u32[]{:S(2)}) collective-permute-start(f32[32,128]{1,0:T(8,128)S(1)} %get-tuple-element.16.refs_1_.refs_0_), channel_id=1, source_target_pairs={{0,12},{1,13},{2,14},{3,15},{4,8},{5,9},{6,10},{7,11},{8,4},{9,5},... | collective-permute-start | bytes 49160 | tf_op jit(solution)/shard_map/ppermute | solution.py:430
  39.6 14.2 %collective-permute-start.4 = (f32[32,128]{1,0:T(8,128)S(1)}, f32[32,128]{1,0:T(8,128)S(1)}, u32[]{:S(2)}, u32[]{:S(2)}) collective-permute-start(f32[32,128]{1,0:T(8,128)S(1)} %get-tuple-element.16.refs_1_.refs_0_), channel_id=1, source_target_pairs={{0,8},{1,9},{2,10},{3,11},{4,12},{5,13},{6,14},{7,15},{8,0},{9,1},... | collective-permute-start | bytes 49160 | tf_op jit(solution)/shard_map/ppermute | solution.py:430
  39.6 14.2 %collective-permute-start.3 = (f32[32,128]{1,0:T(8,128)S(1)}, f32[32,128]{1,0:T(8,128)S(1)}, u32[]{:S(2)}, u32[]{:S(2)}) collective-permute-start(f32[32,128]{1,0:T(8,128)S(1)} %get-tuple-element.16.refs_1_.refs_0_), channel_id=1, source_target_pairs={{0,4},{1,5},{2,6},{3,7},{4,0},{5,1},{6,2},{7,3},{8,12},{9,13},{10,... | collective-permute-start | bytes 49160 | tf_op jit(solution)/shard_map/ppermute | solution.py:430
  52.7 1.1 %copy-start.6 = (s32[6,6]{1,0:T(8,128)S(1)}, s32[6,6]{1,0:T(8,128)}, u32[]{:S(2)}) copy-start(s32[6,6]{1,0:T(8,128)} %far_ref.1) | copy-start | bytes 436
where the time goes:
time: 62.9 us; the launch traced here: 61.7 us
  Pallas kernels  34.4 us (55%)
  starting transfers between devices  19.3 us (31%)
  waiting for transfers between devices  5.42 us (9%)
  local copies, waits for them, and re-layouts  2.39 us (4%)
    pallas_call x5, Pallas kernels, near_part(): pl.pallas_call(functools.partial(near_kernel, feats=feats, region=region,...  19.3 us
    ppermute x4, starting transfers between devices, relatives(): out.append(lax.ppermute(node, 'leaf', pairs))  18.2 us
    pallas_call x1, Pallas kernels, finish(): pl.pallas_call(functools.partial(finish_kernel, feats=feats, base=base, l...  7.86 us
    pallas_call x1, Pallas kernels, prepare(): pl.pallas_call(prepare_kernel, out_shape=(jax.ShapeDtypeStruct((feats + r...  6.56 us
    ppermute x4, waiting for transfers between devices, relatives(): out.append(lax.ppermute(node, 'leaf', pairs))  5.41 us
    unnamed x22, local copies, waits for them, and re-layouts  2.39 us
  transfers between devices with their start and end apart: 6, of which 1 were waited for; matrix products, arithmetic and copies ran while one was open for 0% of the time, Pallas kernels for 32%

commit v1 on v0

--- a/solution.py
+++ b/solution.py
@@ -96,7 +96,7 @@
 
 def prepare_kernel(
     scale_ref, points_ref, charges_ref, order_ref, skel_ref, map_ref, interp_ref,
-    pack_ref, source_ref, target_ref, zs_ref, bs_ref,
+    pack_ref, node_ref, source_ref, target_ref, zs_ref, bs_ref,
 ):
     feats, total = points_ref.shape
     rhs = charges_ref.shape[0]
@@ -150,11 +150,10 @@
         pack_ref[feats:, out] = charge.astype(F32)
         group_q += dot(charge, map_ref[leaf * rank : (leaf + 1) * rank, :])
     columns = [pack_ref[:feats, total + k : total + k + LANES] for k in range(0, leaves * rank, LANES)]
-    node = slice(total + leaves * rank, total + (leaves + 1) * rank)
-    pack_ref[:feats, node] = pick_lanes(
+    node_ref[:feats, :] = pick_lanes(
         columns, lax.broadcasted_iota(jnp.int32, (1, rank), 1) * leaves
     )
-    pack_ref[feats:, node] = group_q
+    node_ref[feats:, :] = group_q
 
 
 def prepare(inv_scale, points, charges, order, skel_idx, interp, group_map):
@@ -166,12 +165,13 @@
     return pl.pallas_call(
         prepare_kernel,
         out_shape=(
-            jax.ShapeDtypeStruct((feats + rhs, total + (leaves + 1) * rank), F32),
+            jax.ShapeDtypeStruct((feats + rhs, total + leaves * rank), F32),
+            jax.ShapeDtypeStruct((feats + rhs, rank), F32),
             jax.ShapeDtypeStruct((stack, total), BF),
             jax.ShapeDtypeStruct((stack, total), BF),
         ),
         in_specs=[SMEM] + [VMEM] * 6,
-        out_specs=(VMEM,) * 3,
+        out_specs=(VMEM,) * 4,
         scratch_shapes=[
             pltpu.VMEM((blocks * feats, 2 * BLOCK), BF),
             pltpu.VMEM((blocks * rhs, BLOCK), BF),
@@ -291,15 +291,14 @@
 
 def climb_kernel(*refs, base, levels, feats):
     count = 2**levels
-    rank = refs[count].shape[1]
-    nodes = [ref[:, ref.shape[1] - rank :] for ref in refs[:count]]
+    nodes = [ref[...] for ref in refs[:count]]
     inters, node = climb(nodes, base, levels, refs[count][...], feats)
     for ref, value in zip(refs[count + 1 :], inters + [node]):
         ref[...] = value
 
 
 def climb_stage(nodes, base, levels, parent_map, feats):
-    rows, rank = nodes[0].shape[0], parent_map.shape[1]
+    rows, rank = nodes[0].shape
     small = jax.ShapeDtypeStruct((rows - feats, rank), F32)
     outs = pl.pallas_call(
         functools.partial(climb_kernel, base=base, levels=levels, feats=feats),
@@ -430,7 +429,7 @@
             out.append(lax.ppermute(node, "leaf", pairs))
         return out
 
-    pack, sources, targets = prepare(
+    pack, node, sources, targets = prepare(
         inv_scale, points, charges, order, skel_idx, interp, group_map
     )
 
@@ -441,19 +440,18 @@
         )
 
     every = near_list.shape[0] * leaves
+    levels = devices.bit_length() - 1
+    stages = [(base, min(2, levels - base)) for base in range(0, levels, 2)]
+    nodes = relatives(node, *stages[0])
+    pack_beyond = lax.ppermute(pack, "leaf", beyond)
     pack_chip = lax.ppermute(pack, "leaf", chip)
-    pack_beyond = lax.ppermute(pack, "leaf", beyond)
-    levels = devices.bit_length() - 1
-    stages = [(1, 1)] + [(base, min(2, levels - base)) for base in range(2, levels, 2)]
     total = near(pack, None, None, 0, (0, 2), 2)
-    inters, node = climb_stage([pack, pack_chip], 0, 1, parent_map, feats)
-    nodes = relatives(node, *stages[0])
-    total = near(pack, total, node, 0, (2, 4), 2)
+    inters = []
     for stage, following in zip(stages[:-1], stages[1:]):
         fresh, node = climb_stage(nodes, *stage, parent_map, feats)
         inters += fresh
         nodes = relatives(node, *following)
-    total = near(pack, total, node, 0, (4, every), 3)
+    total = near(pack, total, node, 0, (2, every), 4)
     total = near(pack_chip, total, None, 1, (0, every), 6)
     total = near(pack_beyond, total, None, 2, (0, every), 6)
     packs = (pack, pack_chip, pack_beyond)

time: 62.9 us -> 52.9 us (0.84)
  the two profiles are of different devices: /device:TPU:0 before, /device:TPU:25 now
where the time goes in v1:
time: 52.9 us; the launch traced here: 53.2 us
  Pallas kernels  33.2 us (63%)
  starting transfers between devices  9.14 us (17%)
  waiting for transfers between devices  8.25 us (16%)
  local copies, waits for them, and re-layouts  2.39 us (5%)
    pallas_call x4, Pallas kernels, near_part(): pl.pallas_call(functools.partial(near_kernel, feats=feats, region=region,...  18.3 us
    ppermute x1, waiting for transfers between devices, body(): pack_beyond = lax.ppermute(pack, 'leaf', beyond)  8.24 us
    pallas_call x1, Pallas kernels, finish(): pl.pallas_call(functools.partial(finish_kernel, feats=feats, base=base, l...  7.86 us
    pallas_call x1, Pallas kernels, prepare(): pl.pallas_call(prepare_kernel, out_shape=(jax.ShapeDtypeStruct((feats + r...  6.55 us
    ppermute x6, starting transfers between devices, relatives(): out.append(lax.ppermute(node, 'leaf', pairs))  5.7 us
    ppermute x1, starting transfers between devices, body(): pack_beyond = lax.ppermute(pack, 'leaf', beyond)  2.74 us
    unnamed x22, local copies, waits for them, and re-layouts  2.39 us
  transfers between devices with their start and end apart: 8, of which 1 were waited for; matrix products, arithmetic and copies ran while one was open for 0% of the time, Pallas kernels for 35%

profile of v1, /device:TPU:25, one launch (start us, length us, event | category | flops | bytes accessed | tf_op | source)
XLA Modules:
  0.0 53.2 jit_solution(954071166582567507)
XLA Ops:
  0.0 0.0 copy-start.8
  0.0 0.7 %copy-done.8 = s32[6144]{0:T(1024)S(1)} copy-done((s32[6144]{0:T(1024)S(1)}, s32[6144]{0:T(1024)}, u32[]{:S(2)}) %copy-start.8) | copy-done | bytes 24600
  0.7 0.0 copy-start
  0.7 0.0 copy-start.1
  0.7 0.0 copy-start.2
  0.7 0.0 copy-start.3
  0.7 0.0 copy-start.5
  0.8 0.0 copy-start.7
  0.8 1.4 %copy-done = bf16[128,6144]{1,0:T(8,128)(2,1)S(1)} copy-done((bf16[128,6144]{1,0:T(8,128)(2,1)S(1)}, bf16[128,6144]{1,0:T(8,128)(2,1)}, u32[]{:S(2)}) %copy-start) | copy-done | bytes 1572888
  2.1 0.0 copy-done.1
  2.1 0.1 copy-done.2
  2.3 0.1 copy-done.3
  2.4 0.0 copy-done.5
  2.4 0.0 copy-done.7
  2.4 0.0 copy-start.9
  2.4 0.0 copy-start.10
  2.4 6.6 %prepare.1 = (f32[32,6912]{1,0:T(8,128)S(1)}, f32[32,128]{1,0:T(8,128)S(1)}, bf16[80,6144]{1,0:T(8,128)(2,1)S(1)}, bf16[80,6144]{1,0:T(8,128)(2,1)S(1)}) custom-call(f32[16]{0:T(128)S(1)} %copy-done.7, f32[16,6144]{1,0:T(8,128)S(1)} %copy-done.2, f32[16,6144]{1,0:T(8,128)S(1)} %copy-done.3, s32[1,6144]{1,0:T(1,128)S(1)} %local_index.1.order_ref, ...), custom_call_target="tpu_custom_call" | custom-call | tf_op jit(solution)/shard_map/prepare/pallas_call | solution.py:165
  9.0 0.7 %collective-permute-start.1 = (f32[32,6912]{1,0:T(8,128)S(1)}, f32[32,6912]{1,0:T(8,128)S(1)}, u32[]{:S(2)}, u32[]{:S(2)}) collective-permute-start(f32[32,6912]{1,0:T(8,128)S(1)} %get-tuple-element.13.src_ref.own_ref), channel_id=1, source_target_pairs={{0,1},{1,0},{2,3},{3,2},{4,5},{5,4},{6,7},{7,6},{8,9},{9,8},{10,11... | collective-permute-start | bytes 2654216 | tf_op jit(solution)/shard_map/ppermute | solution.py:447
  9.7 0.0 collective-permute-start.2
  9.7 1.2 %collective-permute-start.3 = (f32[32,128]{1,0:T(8,128)S(1)}, f32[32,128]{1,0:T(8,128)S(1)}, u32[]{:S(2)}, u32[]{:S(2)}) collective-permute-start(f32[32,128]{1,0:T(8,128)S(1)} %get-tuple-element.15.refs_0_), channel_id=1, source_target_pairs={{0,2},{1,3},{2,0},{3,1},{4,6},{5,7},{6,4},{7,5},{8,10},{9,11},{10,... | collective-permute-start | bytes 49160 | tf_op jit(solution)/shard_map/ppermute | solution.py:429
  10.9 0.9 %collective-permute-start.4 = (f32[32,128]{1,0:T(8,128)S(1)}, f32[32,128]{1,0:T(8,128)S(1)}, u32[]{:S(2)}, u32[]{:S(2)}) collective-permute-start(f32[32,128]{1,0:T(8,128)S(1)} %get-tuple-element.15.refs_0_), channel_id=1, source_target_pairs={{0,3},{1,2},{2,1},{3,0},{4,7},{5,6},{6,5},{7,4},{8,11},{9,10},{10,... | collective-permute-start | bytes 49160 | tf_op jit(solution)/shard_map/ppermute | solution.py:429
  11.8 2.7 %collective-permute-start = (f32[32,6912]{1,0:T(8,128)S(1)}, f32[32,6912]{1,0:T(8,128)S(1)}, u32[]{:S(2)}, u32[]{:S(2)}) collective-permute-start(f32[32,6912]{1,0:T(8,128)S(1)} %get-tuple-element.13.src_ref.own_ref), channel_id=1, source_target_pairs={{1,2},{2,1},{3,4},{4,3},{5,6},{6,5},{7,8},{8,7},{9,10},{10,9},{11,... | collective-permute-start | bytes 2654216 | tf_op jit(solution)/shard_map/ppermute | solution.py:446
  14.6 0.0 copy-done.9
  14.6 0.0 copy-done.10
  14.6 0.0 copy-start.4
  14.6 2.8 %near_0_0.1.refs_0_ = f32[16,6144]{1,0:T(8,128)S(1)} custom-call(s32[3,6]{1,0:T(4,128)S(1)} %bitcast.3, s32[6]{0:T(128)S(1)} %copy-done.10, bf16[80,6144]{1,0:T(8,128)(2,1)S(1)} %get-tuple-element.12.target_ref, f32[32,6912]{1,0:T(8,128)S(1)} %get-tuple-element.13.src_ref.own_ref, bf16[80,6144]{1,0:T(8,128)(2,1)S(1)} %get-tuple-element.14.refs_0_.refs_2_), custom_call_target="tpu_custom_call" | custom-call | flops 2147483648 | bytes 393216 | tf_op jit(solution)/shard_map/near_0_0/pallas_call | solution.py:244
  17.4 0.0 collective-permute-done.2.refs_1_
  17.4 0.0 collective-permute-done.3.refs_2_
  17.4 0.0 collective-permute-done.4.refs_3_
  17.5 0.0 copy-done.4
  17.5 0.5 climb_0.1
  17.9 0.2 collective-permute-start.5
  18.2 0.1 collective-permute-start.6
  18.3 3.2 %collective-permute-start.7 = (f32[32,128]{1,0:T(8,128)S(1)}, f32[32,128]{1,0:T(8,128)S(1)}, u32[]{:S(2)}, u32[]{:S(2)}) collective-permute-start(f32[32,128]{1,0:T(8,128)S(1)} %get-tuple-element.16.refs_1_.refs_0_), channel_id=1, source_target_pairs={{0,12},{1,13},{2,14},{3,15},{4,8},{5,9},{6,10},{7,11},{8,4},{9,5},... | collective-permute-start | bytes 49160 | tf_op jit(solution)/shard_map/ppermute | solution.py:429
  21.5 1.1 %near_0_2.1.refs_0_ = f32[16,6144]{1,0:T(8,128)S(1)} custom-call(s32[3,6]{1,0:T(4,128)S(1)} %bitcast.4, s32[6]{0:T(128)S(1)} %copy-done.10, bf16[80,6144]{1,0:T(8,128)(2,1)S(1)} %get-tuple-element.12.target_ref, f32[32,6912]{1,0:T(8,128)S(1)} %get-tuple-element.13.src_ref.own_ref, f32[16,6144]{1,0:T(8,128)S(1)} %near_0_0.1.refs_0_, ...), custom_call_target="tpu_custom_call" | custom-call | flops 4294967296 | bytes 786432 | tf_op jit(solution)/shard_map/near_0_2/pallas_call | solution.py:244
  22.6 0.0 collective-permute-done.1.src_ref.chip_ref
  22.6 4.8 %near_1_0.1.refs_0_ = f32[16,6144]{1,0:T(8,128)S(1)} custom-call(s32[3,6]{1,0:T(4,128)S(1)} %bitcast.5, s32[6]{0:T(128)S(1)} %copy-done.10, bf16[80,6144]{1,0:T(8,128)(2,1)S(1)} %get-tuple-element.12.target_ref, f32[32,6912]{1,0:T(8,128)S(1)} %collective-permute-done.1.src_ref.chip_ref, f32[16,6144]{1,0:T(8,128)S(1)} %near_0_2.1.refs_0_), custom_call_target="tpu_custom_call" | custom-call | flops 6442450944 | bytes 1179648 | tf_op jit(solution)/shard_map/near_1_0/pallas_call | solution.py:244
  27.4 0.0 copy-start.6
  27.4 8.2 %collective-permute-done.src_ref.beyond_ref = f32[32,6912]{1,0:T(8,128)S(1)} collective-permute-done((f32[32,6912]{1,0:T(8,128)S(1)}, f32[32,6912]{1,0:T(8,128)S(1)}, u32[]{:S(2)}, u32[]{:S(2)}) %collective-permute-start) | collective-permute-done | bytes 884768 | tf_op jit(solution)/shard_map/ppermute | solution.py:446
  35.7 9.6 %near_2_0.1.near_ref = f32[16,6144]{1,0:T(8,128)S(1)} custom-call(s32[3,6]{1,0:T(4,128)S(1)} %bitcast.6, s32[6]{0:T(128)S(1)} %copy-done.10, bf16[80,6144]{1,0:T(8,128)(2,1)S(1)} %get-tuple-element.12.target_ref, f32[32,6912]{1,0:T(8,128)S(1)} %collective-permute-done.src_ref.beyond_ref, f32[16,6144]{1,0:T(8,128)S(1)} %near_1_0.1.refs_0_), custom_call_target="tpu_custom_call" | custom-call | flops 6442450944 | bytes 1179648 | tf_op jit(solution)/shard_map/near_2_0/pallas_call | solution.py:244
  45.3 0.0 collective-permute-done.5.refs_1_
  45.3 0.0 collective-permute-done.6.refs_2_
  45.3 0.0 collective-permute-done.7.refs_3_
  45.3 0.0 copy-done.6
  45.3 7.9 %finish.1 = f32[16,6144]{1,0:T(8,128)} custom-call(s32[6,6]{1,0:T(8,128)S(1)} %copy-done.6, f32[16,6144]{1,0:T(8,128)S(1)} %near_2_0.1.near_ref, f32[32,6912]{1,0:T(8,128)S(1)} %get-tuple-element.13.src_ref.own_ref, f32[32,6912]{1,0:T(8,128)S(1)} %collective-permute-done.1.src_ref.chip_ref, f32[32,6912]{1,0:T(8,128)S(1)} %collective-permute-done.src_ref.beyond_ref, ...), custom_call_target="tpu_custom_call" | custom-call | tf_op jit(solution)/shard_map/finish/pallas_call | solution.py:387
  (1 shorter events, 0.0 us)
Async XLA Ops:
  0.0 0.7 %copy-start.8 = (s32[6144]{0:T(1024)S(1)}, s32[6144]{0:T(1024)}, u32[]{:S(2)}) copy-start(s32[6144]{0:T(1024)} %param.14) | copy-start | bytes 73732
  0.7 1.4 %copy-start = (bf16[128,6144]{1,0:T(8,128)(2,1)S(1)}, bf16[128,6144]{1,0:T(8,128)(2,1)}, u32[]{:S(2)}) copy-start(bf16[128,6144]{1,0:T(8,128)(2,1)} %interp_ref.3) | copy-start | bytes 4718596
  0.7 1.4 %copy-start.1 = (bf16[768,128]{1,0:T(8,128)(2,1)S(1)}, bf16[768,128]{1,0:T(8,128)(2,1)}, u32[]{:S(2)}) copy-start(bf16[768,128]{1,0:T(8,128)(2,1)} %map_ref.3) | copy-start | bytes 589828
  0.7 1.5 %copy-start.2 = (f32[16,6144]{1,0:T(8,128)S(1)}, f32[16,6144]{1,0:T(8,128)}, u32[]{:S(2)}) copy-start(f32[16,6144]{1,0:T(8,128)} %points_ref.1) | copy-start | bytes 1179652
  0.7 1.7 %copy-start.3 = (f32[16,6144]{1,0:T(8,128)S(1)}, f32[16,6144]{1,0:T(8,128)}, u32[]{:S(2)}) copy-start(f32[16,6144]{1,0:T(8,128)} %charges_ref.1) | copy-start | bytes 1179652
  0.7 1.7 %copy-start.5 = (s32[6,128]{1,0:T(8,128)S(1)}, s32[6,128]{1,0:T(8,128)}, u32[]{:S(2)}) copy-start(s32[6,128]{1,0:T(8,128)} %skel_ref.1) | copy-start | bytes 9220
  0.8 1.7 %copy-start.7 = (f32[16]{0:T(128)S(1)}, f32[16]{0:T(128)}, u32[]{:S(2)}) copy-start(f32[16]{0:T(128)} %scale_ref.1) | copy-start | bytes 196
  2.4 12.2 %copy-start.9 = (s32[6,3]{0,1:T(4,128)S(1)}, s32[6,3]{0,1:T(4,128)}, u32[]{:S(2)}) copy-start(s32[6,3]{0,1:T(4,128)} %param.15) | copy-start | bytes 220
  2.4 12.2 %copy-start.10 = (s32[6]{0:T(128)S(1)}, s32[6]{0:T(128)}, u32[]{:S(2)}) copy-start(s32[6]{0:T(128)} %count_ref.7) | copy-start | bytes 76
  9.0 13.6 %collective-permute-start.1 = (f32[32,6912]{1,0:T(8,128)S(1)}, f32[32,6912]{1,0:T(8,128)S(1)}, u32[]{:S(2)}, u32[]{:S(2)}) collective-permute-start(f32[32,6912]{1,0:T(8,128)S(1)} %get-tuple-element.13.src_ref.own_ref), channel_id=1, source_target_pairs={{0,1},{1,0},{2,3},{3,2},{4,5},{5,4},{6,7},{7,6},{8,9},{9,8},{10,11... | collective-permute-start | bytes 2654216 | tf_op jit(solution)/shard_map/ppermute | solution.py:447
  9.7 7.7 %collective-permute-start.2 = (f32[32,128]{1,0:T(8,128)S(1)}, f32[32,128]{1,0:T(8,128)S(1)}, u32[]{:S(2)}, u32[]{:S(2)}) collective-permute-start(f32[32,128]{1,0:T(8,128)S(1)} %get-tuple-element.15.refs_0_), channel_id=1, source_target_pairs={{0,1},{1,0},{2,3},{3,2},{4,5},{5,4},{6,7},{7,6},{8,9},{9,8},{10,11... | collective-permute-start | bytes 49160 | tf_op jit(solution)/shard_map/ppermute | solution.py:429
  9.7 7.8 %collective-permute-start.3 = (f32[32,128]{1,0:T(8,128)S(1)}, f32[32,128]{1,0:T(8,128)S(1)}, u32[]{:S(2)}, u32[]{:S(2)}) collective-permute-start(f32[32,128]{1,0:T(8,128)S(1)} %get-tuple-element.15.refs_0_), channel_id=1, source_target_pairs={{0,2},{1,3},{2,0},{3,1},{4,6},{5,7},{6,4},{7,5},{8,10},{9,11},{10,... | collective-permute-start | bytes 49160 | tf_op jit(solution)/shard_map/ppermute | solution.py:429
  10.9 6.5 %collective-permute-start.4 = (f32[32,128]{1,0:T(8,128)S(1)}, f32[32,128]{1,0:T(8,128)S(1)}, u32[]{:S(2)}, u32[]{:S(2)}) collective-permute-start(f32[32,128]{1,0:T(8,128)S(1)} %get-tuple-element.15.refs_0_), channel_id=1, source_target_pairs={{0,3},{1,2},{2,1},{3,0},{4,7},{5,6},{6,5},{7,4},{8,11},{9,10},{10,... | collective-permute-start | bytes 49160 | tf_op jit(solution)/shard_map/ppermute | solution.py:429
  11.8 23.8 %collective-permute-start = (f32[32,6912]{1,0:T(8,128)S(1)}, f32[32,6912]{1,0:T(8,128)S(1)}, u32[]{:S(2)}, u32[]{:S(2)}) collective-permute-start(f32[32,6912]{1,0:T(8,128)S(1)} %get-tuple-element.13.src_ref.own_ref), channel_id=1, source_target_pairs={{1,2},{2,1},{3,4},{4,3},{5,6},{6,5},{7,8},{8,7},{9,10},{10,9},{11,... | collective-permute-start | bytes 2654216 | tf_op jit(solution)/shard_map/ppermute | solution.py:446
  14.6 2.9 %copy-start.4 = (bf16[256,128]{1,0:T(8,128)(2,1)S(1)}, bf16[256,128]{1,0:T(8,128)(2,1)}, u32[]{:S(2)}) copy-start(bf16[256,128]{1,0:T(8,128)(2,1)} %parent_ref.1) | copy-start | bytes 196612
  17.9 27.3 %collective-permute-start.5 = (f32[32,128]{1,0:T(8,128)S(1)}, f32[32,128]{1,0:T(8,128)S(1)}, u32[]{:S(2)}, u32[]{:S(2)}) collective-permute-start(f32[32,128]{1,0:T(8,128)S(1)} %get-tuple-element.16.refs_1_.refs_0_), channel_id=1, source_target_pairs={{0,4},{1,5},{2,6},{3,7},{4,0},{5,1},{6,2},{7,3},{8,12},{9,13},{10,... | collective-permute-start | bytes 49160 | tf_op jit(solution)/shard_map/ppermute | solution.py:429
  18.2 27.1 %collective-permute-start.6 = (f32[32,128]{1,0:T(8,128)S(1)}, f32[32,128]{1,0:T(8,128)S(1)}, u32[]{:S(2)}, u32[]{:S(2)}) collective-permute-start(f32[32,128]{1,0:T(8,128)S(1)} %get-tuple-element.16.refs_1_.refs_0_), channel_id=1, source_target_pairs={{0,8},{1,9},{2,10},{3,11},{4,12},{5,13},{6,14},{7,15},{8,0},{9,1},... | collective-permute-start | bytes 49160 | tf_op jit(solution)/shard_map/ppermute | solution.py:429
  18.3 27.0 %collective-permute-start.7 = (f32[32,128]{1,0:T(8,128)S(1)}, f32[32,128]{1,0:T(8,128)S(1)}, u32[]{:S(2)}, u32[]{:S(2)}) collective-permute-start(f32[32,128]{1,0:T(8,128)S(1)} %get-tuple-element.16.refs_1_.refs_0_), channel_id=1, source_target_pairs={{0,12},{1,13},{2,14},{3,15},{4,8},{5,9},{6,10},{7,11},{8,4},{9,5},... | collective-permute-start | bytes 49160 | tf_op jit(solution)/shard_map/ppermute | solution.py:429
  27.4 17.9 %copy-start.6 = (s32[6,6]{1,0:T(8,128)S(1)}, s32[6,6]{1,0:T(8,128)}, u32[]{:S(2)}) copy-start(s32[6,6]{1,0:T(8,128)} %far_ref.1) | copy-start | bytes 436
